TPU v7x, 32 devices: a whole 2x2x4 slice. The times are simulated.
32 devices in a mesh: tm: 2 (over x), height: 16 (over z, y, core).
Axes of the slice: x: 2, y: 2, z: 4, core: 2. Of those that a mesh axis runs over, the one named last changes fastest.
Arguments:
- features: bfloat16 [96, 8, 64, 128], P(None, 'tm', 'height'), may hold values from -6 to 6
- first_gain: float32 [96], replicated, may hold values from 0.1 to 1.9
- first_weight: bfloat16 [96, 2592], replicated, may hold values from -0.125 to 0.125
- first_bias: float32 [96], replicated, may hold values from -3 to 3
- second_gain: float32 [96], replicated, may hold values from 0.1 to 1.9
- second_weight: bfloat16 [96, 2592], replicated, may hold values from -0.125 to 0.125
- second_bias: float32 [96], replicated, may hold values from -3 to 3
Outputs:
- encoded: bfloat16 [96, 8, 64, 128], P(None, 'tm', 'height')
All inputs are finite; a program needn't handle non-finite values.
Results may differ from a plain program's by a relative error of at most 0.0036.
Values may be sent and summed in bfloat16 or wider, within the bound.
A program may use at most 64 MiB of HBM per device.

v0:
```python
import jax
import jax.numpy as jnp
from jax import lax
from jax.sharding import PartitionSpec as P


def with_halo(block, sides, width):
    for axis, dim in sides:
        count = lax.axis_size(axis)
        forward = [(i, i + 1) for i in range(count - 1)]
        backward = [(target, source) for source, target in forward]
        low = lax.ppermute(
            lax.slice_in_dim(block, block.shape[dim] - width, None, axis=dim), axis, forward
        )
        high = lax.ppermute(lax.slice_in_dim(block, 0, width, axis=dim), axis, backward)
        block = jnp.concatenate([low, block, high], axis=dim)
    return block


def shifted(block, axis, distance):
    devices = range(lax.axis_size(axis))
    route = [(i - distance, i) for i in devices if i - distance in devices]
    return lax.ppermute(block, axis, route)


def activate(values, gain_vector):
    mean_square = jnp.mean(values * values, axis=0, keepdims=True)
    scaled = values * lax.rsqrt(mean_square + 1e-06) * gain_vector[:, None, None, None]
    return jax.nn.silu(scaled).astype(jnp.bfloat16)


def widen_rows(extended):
    return with_halo(extended, (("height", 2),), 1)


def valid_conv(padded, weight, bias_vector):
    channels = weight.shape[0]
    frames_out = padded.shape[1] - 2
    rows_out = padded.shape[2] - 2
    columns = padded.shape[3]
    widened = jnp.pad(padded, ((0, 0), (0, 0), (0, 0), (1, 1)))
    running = jnp.broadcast_to(
        bias_vector[:, None, None, None], (channels, frames_out, rows_out, columns)
    )
    for time_tap in range(3):
        window = widened[:, time_tap : time_tap + frames_out]
        stacked = jnp.concatenate(
            [window[..., column_tap : column_tap + columns] for column_tap in range(3)], axis=0
        )
        for row_tap in range(3):
            offset = (time_tap * 3 + row_tap) * 3 * channels
            tap_weight = weight[:, offset : offset + 3 * channels]
            running = running + jnp.einsum(
                "oi,ifrw->ofrw",
                tap_weight,
                stacked[:, :, row_tap : row_tap + rows_out],
                preferred_element_type=jnp.float32,
            )
    return running


def layer_conv(inputs, weight, bias_vector):
    earlier = shifted(inputs[:, -2:], "tm", 1)
    padded = widen_rows(jnp.concatenate([earlier, inputs], axis=1))
    return valid_conv(padded, weight, bias_vector)


def local(features, first_gain, first_weight, first_bias, second_gain, second_weight, second_bias):
    first_act = activate(features.astype(jnp.float32), first_gain)
    hidden = layer_conv(first_act, first_weight, first_bias)
    second_act = activate(hidden, second_gain)
    branch = layer_conv(second_act, second_weight, second_bias)
    return (features.astype(jnp.float32) + branch).astype(jnp.bfloat16)


def solution(mesh):
    return jax.shard_map(
        local,
        mesh=mesh,
        in_specs=(P(None, "tm", "height", None), P(), P(), P(), P(), P(), P()),
        out_specs=P(None, "tm", "height", None),
        check_vma=False,
    )
```

profile of v0, /device:TPU:23, one launch (start us, length us, event | category | flops | bytes accessed | tf_op | source)
XLA Modules:
  0.0 56.4 jit_solution(7559664317786091856)
XLA Ops:
  0.0 1.1 %fusion.21 = f32[4,4,128]{2,1,0:T(4,128)S(1)} fusion(bf16[96,4,4,128]{3,2,1,0:T(4,128)(2,1)} %param.7), kind=kLoop, calls=%fused_computation.61 | loop fusion | flops 587776 | bytes 401408 | tf_op jit(solution)/shard_map/reduce_sum | solution.py:27
  1.1 1.3 %fusion.28 = bf16[96,4,4,128]{3,0,2,1:T(8,128)(2,1)S(1)} fusion(f32[96]{0:T(128)} %param.8, f32[4,4,128]{2,1,0:T(4,128)S(1)} %add_rsqrt_fusion.1, bf16[96,4,4,128]{3,2,1,0:T(4,128)(2,1)} %param.7), kind=kLoop, calls=%fused_computation.68 | loop fusion | flops 1572864 | bytes 795008 | tf_op jit(solution)/shard_map/convert_element_type | solution.py:29
  2.5 1.3 %collective-permute-start = (bf16[96,2,4,128]{3,0,2,1:T(8,128)(2,1)S(1)}, bf16[96,2,4,128]{3,0,2,1:T(8,128)(2,1)S(1)}, u32[]{:S(2)}, u32[]{:S(2)}) collective-permute-start(bf16[96,2,4,128]{3,0,2,1:T(8,128)(2,1)S(1)} %slice.270), channel_id=1, source_target_pairs={{0,16},{1,17},{2,18},{3,19},{4,20},{5,21},{6,22},{7,23},{8,24},{9,... | collective-permute-start | bytes 589832 | tf_op jit(solution)/shard_map/ppermute | solution.py:23
  3.8 6.4 %collective-permute-done = bf16[96,2,4,128]{3,0,2,1:T(8,128)(2,1)S(1)} collective-permute-done((bf16[96,2,4,128]{3,0,2,1:T(8,128)(2,1)S(1)}, bf16[96,2,4,128]{3,0,2,1:T(8,128)(2,1)S(1)}, u32[]{:S(2)}, u32[]{:S(2)}) %collective-permute-start) | collective-permute-done | bytes 196640 | tf_op jit(solution)/shard_map/ppermute | solution.py:23
  10.2 4.6 %collective-permute-start.1 = (bf16[96,6,1,128]{3,0,2,1:T(8,128)(2,1)S(1)}, bf16[96,6,1,128]{3,0,2,1:T(8,128)(2,1)S(1)}, u32[]{:S(2)}, u32[]{:S(2)}) collective-permute-start(bf16[96,6,1,128]{3,0,2,1:T(8,128)(2,1)S(1)} %get-tuple-element.25), channel_id=1, source_target_pairs={{0,1},{1,2},{2,3},{3,4},{4,5},{5,6},{6,7},{7,8},{8,9},{9,10},{10,1... | collective-permute-start | bytes 442376 | tf_op jit(solution)/shard_map/ppermute | solution.py:12
  14.8 1.9 %collective-permute-start.2 = (bf16[96,6,1,128]{3,0,2,1:T(8,128)(2,1)S(1)}, bf16[96,6,1,128]{3,0,2,1:T(8,128)(2,1)S(1)}, u32[]{:S(2)}, u32[]{:S(2)}) collective-permute-start(bf16[96,6,1,128]{3,0,2,1:T(8,128)(2,1)S(1)} %get-tuple-element.26), channel_id=1, source_target_pairs={{1,0},{2,1},{3,2},{4,3},{5,4},{6,5},{7,6},{8,7},{9,8},{10,9},{11,1... | collective-permute-start | bytes 442376 | tf_op jit(solution)/shard_map/ppermute | solution.py:15
  16.8 5.3 %collective-permute-done.2 = bf16[96,6,1,128]{3,0,2,1:T(8,128)(2,1)S(1)} collective-permute-done((bf16[96,6,1,128]{3,0,2,1:T(8,128)(2,1)S(1)}, bf16[96,6,1,128]{3,0,2,1:T(8,128)(2,1)S(1)}, u32[]{:S(2)}, u32[]{:S(2)}) %collective-permute-start.2) | collective-permute-done | bytes 147488 | tf_op jit(solution)/shard_map/ppermute | solution.py:15
  22.3 1.2 %pad_slice_fusion.7 = (bf16[96,4,6,128]{3,0,2,1:T(8,128)(2,1)S(1)}, bf16[96,4,6,128]{3,0,2,1:T(8,128)(2,1)S(1)}, bf16[96,4,6,128]{3,0,2,1:T(8,128)(2,1)S(1)}, bf...) fusion(bf16[96,6,6,128]{3,0,2,1:T(8,128)(2,1)S(1)} %pad_maximum, ...), kind=kLoop, calls=%fused_computation.7 | loop fusion | bytes 7962624 | tf_op jit(solution)/shard_map/slice | solution.py:48
  23.8 0.7 %copy-done.1 = bf16[96,2592]{1,0:T(8,128)(2,1)S(1)} copy-done((bf16[96,2592]{1,0:T(8,128)(2,1)S(1)}, bf16[96,2592]{1,0:T(8,128)(2,1)}, u32[]{:S(2)}) %copy-start.1) | copy-done | bytes 497688
  25.0 0.5 convolution_add_fusion.16
  25.4 0.5 convolution_add_fusion.15
  25.9 0.5 convolution_add_fusion.14
  26.4 0.4 convolution_add_fusion.13
  26.8 0.5 convolution_add_fusion.12
  27.4 0.5 convolution_add_fusion.11
  27.9 0.5 convolution_add_fusion.10
  28.4 0.4 multiply_reduce_fusion
  29.4 1.3 %collective-permute-start.3 = (bf16[96,2,4,128]{3,0,2,1:T(8,128)(2,1)S(1)}, bf16[96,2,4,128]{3,0,2,1:T(8,128)(2,1)S(1)}, u32[]{:S(2)}, u32[]{:S(2)}) collective-permute-start(bf16[96,2,4,128]{3,0,2,1:T(8,128)(2,1)S(1)} %slice.283), channel_id=1, source_target_pairs={{0,16},{1,17},{2,18},{3,19},{4,20},{5,21},{6,22},{7,23},{8,24},{9,... | collective-permute-start | bytes 589832 | tf_op jit(solution)/shard_map/ppermute | solution.py:23
  30.7 5.5 %collective-permute-done.3 = bf16[96,2,4,128]{3,0,2,1:T(8,128)(2,1)S(1)} collective-permute-done((bf16[96,2,4,128]{3,0,2,1:T(8,128)(2,1)S(1)}, bf16[96,2,4,128]{3,0,2,1:T(8,128)(2,1)S(1)}, u32[]{:S(2)}, u32[]{:S(2)}) %collective-permute-start.3) | collective-permute-done | bytes 196640 | tf_op jit(solution)/shard_map/ppermute | solution.py:23
  36.2 4.5 %collective-permute-start.4 = (bf16[96,6,1,128]{3,0,2,1:T(8,128)(2,1)S(1)}, bf16[96,6,1,128]{3,0,2,1:T(8,128)(2,1)S(1)}, u32[]{:S(2)}, u32[]{:S(2)}) collective-permute-start(bf16[96,6,1,128]{3,0,2,1:T(8,128)(2,1)S(1)} %get-tuple-element.23), channel_id=1, source_target_pairs={{0,1},{1,2},{2,3},{3,4},{4,5},{5,6},{6,7},{7,8},{8,9},{9,10},{10,1... | collective-permute-start | bytes 442376 | tf_op jit(solution)/shard_map/ppermute | solution.py:12
  40.8 1.9 %collective-permute-start.5 = (bf16[96,6,1,128]{3,0,2,1:T(8,128)(2,1)S(1)}, bf16[96,6,1,128]{3,0,2,1:T(8,128)(2,1)S(1)}, u32[]{:S(2)}, u32[]{:S(2)}) collective-permute-start(bf16[96,6,1,128]{3,0,2,1:T(8,128)(2,1)S(1)} %get-tuple-element.24), channel_id=1, source_target_pairs={{1,0},{2,1},{3,2},{4,3},{5,4},{6,5},{7,6},{8,7},{9,8},{10,9},{11,1... | collective-permute-start | bytes 442376 | tf_op jit(solution)/shard_map/ppermute | solution.py:15
  42.8 5.3 %collective-permute-done.5 = bf16[96,6,1,128]{3,0,2,1:T(8,128)(2,1)S(1)} collective-permute-done((bf16[96,6,1,128]{3,0,2,1:T(8,128)(2,1)S(1)}, bf16[96,6,1,128]{3,0,2,1:T(8,128)(2,1)S(1)}, u32[]{:S(2)}, u32[]{:S(2)}) %collective-permute-start.5) | collective-permute-done | bytes 147488 | tf_op jit(solution)/shard_map/ppermute | solution.py:15
  48.2 1.2 %pad_slice_fusion.1 = (bf16[96,4,6,128]{3,0,2,1:T(8,128)(2,1)S(1)}, bf16[96,4,6,128]{3,0,2,1:T(8,128)(2,1)S(1)}, bf16[96,4,6,128]{3,0,2,1:T(8,128)(2,1)S(1)}, bf...) fusion(bf16[96,6,6,128]{3,0,2,1:T(8,128)(2,1)S(1)} %pad_maximum, ...), kind=kLoop, calls=%fused_computation.1 | loop fusion | bytes 7962624 | tf_op jit(solution)/shard_map/slice | solution.py:48
  49.6 0.9 %copy-done.2 = bf16[96,2592]{1,0:T(8,128)(2,1)S(1)} copy-done((bf16[96,2592]{1,0:T(8,128)(2,1)S(1)}, bf16[96,2592]{1,0:T(8,128)(2,1)}, u32[]{:S(2)}) %copy-start.2) | copy-done | bytes 497688
  51.0 0.5 convolution_add_fusion.7
  51.4 0.5 convolution_add_fusion.6
  52.0 0.5 convolution_add_fusion.5
  52.9 0.5 convolution_add_fusion.3
  53.5 0.5 convolution_add_fusion.2
  54.0 0.5 convolution_add_fusion.1
  54.5 0.5 copy-done
  55.4 0.9 %copy.9 = bf16[96,4,4,128]{3,2,1,0:T(4,128)(2,1)} copy(bf16[96,4,4,128]{3,0,2,1:T(8,128)(2,1)S(1)} %fusion.2) | data formatting | bytes 786432 | tf_op jit(solution)/shard_map/convert_element_type | solution.py:73
  (29 shorter events, 3.7 us)
Async XLA Ops:
  2.5 7.7 %collective-permute-start = (bf16[96,2,4,128]{3,0,2,1:T(8,128)(2,1)S(1)}, bf16[96,2,4,128]{3,0,2,1:T(8,128)(2,1)S(1)}, u32[]{:S(2)}, u32[]{:S(2)}) collective-permute-start(bf16[96,2,4,128]{3,0,2,1:T(8,128)(2,1)S(1)} %slice.270), channel_id=1, source_target_pairs={{0,16},{1,17},{2,18},{3,19},{4,20},{5,21},{6,22},{7,23},{8,24},{9,... | collective-permute-start | bytes 589832 | tf_op jit(solution)/shard_map/ppermute | solution.py:23
  10.2 6.7 %collective-permute-start.1 = (bf16[96,6,1,128]{3,0,2,1:T(8,128)(2,1)S(1)}, bf16[96,6,1,128]{3,0,2,1:T(8,128)(2,1)S(1)}, u32[]{:S(2)}, u32[]{:S(2)}) collective-permute-start(bf16[96,6,1,128]{3,0,2,1:T(8,128)(2,1)S(1)} %get-tuple-element.25), channel_id=1, source_target_pairs={{0,1},{1,2},{2,3},{3,4},{4,5},{5,6},{6,7},{7,8},{8,9},{9,10},{10,1... | collective-permute-start | bytes 442376 | tf_op jit(solution)/shard_map/ppermute | solution.py:12
  14.8 7.4 %collective-permute-start.2 = (bf16[96,6,1,128]{3,0,2,1:T(8,128)(2,1)S(1)}, bf16[96,6,1,128]{3,0,2,1:T(8,128)(2,1)S(1)}, u32[]{:S(2)}, u32[]{:S(2)}) collective-permute-start(bf16[96,6,1,128]{3,0,2,1:T(8,128)(2,1)S(1)} %get-tuple-element.26), channel_id=1, source_target_pairs={{1,0},{2,1},{3,2},{4,3},{5,4},{6,5},{7,6},{8,7},{9,8},{10,9},{11,1... | collective-permute-start | bytes 442376 | tf_op jit(solution)/shard_map/ppermute | solution.py:15
  23.5 1.0 %copy-start.1 = (bf16[96,2592]{1,0:T(8,128)(2,1)S(1)}, bf16[96,2592]{1,0:T(8,128)(2,1)}, u32[]{:S(2)}) copy-start(bf16[96,2592]{1,0:T(8,128)(2,1)} %param.9) | copy-start | bytes 1492996
  23.5 1.0 %copy-start.3 = (f32[96]{0:T(128)S(1)}, f32[96]{0:T(128)}, u32[]{:S(2)}) copy-start(f32[96]{0:T(128)} %param.10) | copy-start | bytes 1156
  28.4 0.7 %copy-start.4 = (f32[96]{0:T(128)S(1)}, f32[96]{0:T(128)}, u32[]{:S(2)}) copy-start(f32[96]{0:T(128)} %param.11) | copy-start | bytes 1156
  29.4 6.8 %collective-permute-start.3 = (bf16[96,2,4,128]{3,0,2,1:T(8,128)(2,1)S(1)}, bf16[96,2,4,128]{3,0,2,1:T(8,128)(2,1)S(1)}, u32[]{:S(2)}, u32[]{:S(2)}) collective-permute-start(bf16[96,2,4,128]{3,0,2,1:T(8,128)(2,1)S(1)} %slice.283), channel_id=1, source_target_pairs={{0,16},{1,17},{2,18},{3,19},{4,20},{5,21},{6,22},{7,23},{8,24},{9,... | collective-permute-start | bytes 589832 | tf_op jit(solution)/shard_map/ppermute | solution.py:23
  36.2 6.6 %collective-permute-start.4 = (bf16[96,6,1,128]{3,0,2,1:T(8,128)(2,1)S(1)}, bf16[96,6,1,128]{3,0,2,1:T(8,128)(2,1)S(1)}, u32[]{:S(2)}, u32[]{:S(2)}) collective-permute-start(bf16[96,6,1,128]{3,0,2,1:T(8,128)(2,1)S(1)} %get-tuple-element.23), channel_id=1, source_target_pairs={{0,1},{1,2},{2,3},{3,4},{4,5},{5,6},{6,7},{7,8},{8,9},{9,10},{10,1... | collective-permute-start | bytes 442376 | tf_op jit(solution)/shard_map/ppermute | solution.py:12
  40.8 7.4 %collective-permute-start.5 = (bf16[96,6,1,128]{3,0,2,1:T(8,128)(2,1)S(1)}, bf16[96,6,1,128]{3,0,2,1:T(8,128)(2,1)S(1)}, u32[]{:S(2)}, u32[]{:S(2)}) collective-permute-start(bf16[96,6,1,128]{3,0,2,1:T(8,128)(2,1)S(1)} %get-tuple-element.24), channel_id=1, source_target_pairs={{1,0},{2,1},{3,2},{4,3},{5,4},{6,5},{7,6},{8,7},{9,8},{10,9},{11,1... | collective-permute-start | bytes 442376 | tf_op jit(solution)/shard_map/ppermute | solution.py:15
  49.5 1.0 %copy-start.2 = (bf16[96,2592]{1,0:T(8,128)(2,1)S(1)}, bf16[96,2592]{1,0:T(8,128)(2,1)}, u32[]{:S(2)}) copy-start(bf16[96,2592]{1,0:T(8,128)(2,1)} %param.12) | copy-start | bytes 1492996
  49.5 1.0 %copy-start.5 = (f32[96]{0:T(128)S(1)}, f32[96]{0:T(128)}, u32[]{:S(2)}) copy-start(f32[96]{0:T(128)} %param.13) | copy-start | bytes 1156
  54.0 1.0 %copy-start = (bf16[96,4,4,128]{3,2,1,0:T(4,128)(2,1)S(1)}, bf16[96,4,4,128]{3,2,1,0:T(4,128)(2,1)}, u32[]{:S(2)}) copy-start(bf16[96,4,4,128]{3,2,1,0:T(4,128)(2,1)} %param.7) | copy-start | bytes 1179652
where the time goes:
time: 56.7 us; the launch traced here: 56.4 us
  waiting for transfers between devices  22.7 us (40%)
  starting transfers between devices  15.5 us (27%)
  matrix products  8.19 us (14%)
  local copies, waits for them, and re-layouts  5.75 us (10%)
  other arithmetic  3.87 us (7%)
    ppermute x2, waiting for transfers between devices, shifted(): return lax.ppermute(block, axis, route)  11.9 us
    ppermute x2, waiting for transfers between devices, with_halo(): lax.ppermute(lax.slice_in_dim(block, 0, width, axis=dim), axis, backward)  10.6 us
    ppermute x2, starting transfers between devices, with_halo(): lax.ppermute(lax.slice_in_dim(block, block.shape[dim] - width, None, axis...  9.12 us
    dot_general x18, matrix products, valid_conv(): jnp.einsum('oi,ifrw->ofrw', tap_weight, stacked[:, :, row_tap:row_tap + r...  8.19 us
    ppermute x2, starting transfers between devices, with_halo(): lax.ppermute(lax.slice_in_dim(block, 0, width, axis=dim), axis, backward)  3.84 us
    ppermute x2, starting transfers between devices, shifted(): return lax.ppermute(block, axis, route)  2.58 us
    slice x2, local copies, waits for them, and re-layouts, valid_conv(): window[..., column_tap:column_tap + columns]  2.47 us
    unnamed x12, local copies, waits for them, and re-layouts  2.3 us
  transfers between devices with their start and end apart: 6, of which 6 were waited for; matrix products, arithmetic and copies ran while one was open for 0% of the time, Pallas kernels for 0%

commit v1 on v0

v1 whole, which is shorter than its diff:
```python
import functools

import jax
import jax.numpy as jnp
from jax import lax
from jax.experimental import pallas as pl
from jax.experimental.pallas import tpu as pltpu
from jax.sharding import PartitionSpec as P

MESH = pl.DeviceIdType.MESH
ROW_PAIRS = ((1, 2), (0, 3))


def activate(values, gain):
    mean_square = jnp.mean(values * values, axis=0, keepdims=True)
    scaled = values * lax.rsqrt(mean_square + 1e-06) * gain
    return scaled / (1.0 + jnp.exp(-scaled))


def spread(taps, frame, row, values):
    lanes = lax.broadcasted_iota(jnp.int32, values.shape, 1)
    last = values.shape[1] - 1
    before = jnp.where(lanes == 0, 0.0, pltpu.roll(values, 1, 1))
    after = jnp.where(lanes == last, 0.0, pltpu.roll(values, last, 1))
    taps[frame, row, 0] = before.astype(jnp.bfloat16)
    taps[frame, row, 1] = values.astype(jnp.bfloat16)
    taps[frame, row, 2] = after.astype(jnp.bfloat16)


def add_frame(total, taps, weights, frame, pair):
    channels = taps.shape[3]
    columns = taps.shape[4]
    reached = [(tap, frame + 2 - tap) for tap in range(3) if 0 <= frame + 2 - tap < 4]
    low = reached[0][0] * channels
    right = jnp.concatenate(
        [taps[frame + 2, r : r + 3].reshape(9 * channels, columns) for r in pair], axis=1
    )
    part = jnp.dot(
        weights[low : low + len(reached) * channels, :],
        right,
        preferred_element_type=jnp.float32,
    )
    for i, (_, target) in enumerate(reached):
        for j, r in enumerate(pair):
            total[target, r] += part[
                i * channels : (i + 1) * channels, j * columns : (j + 1) * columns
            ]


def kernel(
    tm_count,
    height_count,
    features,
    vectors,
    first_weight,
    second_weight,
    out,
    weights_a,
    weights_b,
    own,
    above,
    below,
    earlier,
    earlier_above,
    earlier_below,
    taps_a,
    taps_b,
    total,
    send_sem,
    recv_sem,
):
    t = lax.axis_index("tm")
    h = lax.axis_index("height")
    has_prev, has_next = t > 0, t < tm_count - 1
    has_up, has_down = h > 0, h < height_count - 1
    up, down = (t, h - 1), (t, h + 1)
    later = (t + 1, h)

    barrier = pltpu.get_barrier_semaphore()
    neighbours = (
        (has_prev, (t - 1, h)),
        (has_next, later),
        (has_up, up),
        (has_down, down),
    )
    for present, device in neighbours:

        @pl.when(present)
        def _():
            pl.semaphore_signal(barrier, inc=1, device_id=device, device_id_type=MESH)

    def message(layer, slot, source, target, device):
        return pltpu.make_async_remote_copy(
            src_ref=source,
            dst_ref=target,
            send_sem=send_sem.at[layer, slot],
            recv_sem=recv_sem.at[layer, slot],
            device_id=device,
            device_id_type=MESH,
        )

    def to_up(layer, half):
        frames = pl.ds(2 * half, 2)
        return message(
            layer, half, own.at[layer, frames, 0], below.at[layer, frames], up
        )

    def to_down(layer, half):
        frames = pl.ds(2 * half, 2)
        return message(
            layer, 2 + half, own.at[layer, frames, 3], above.at[layer, frames], down
        )

    def to_later(layer, part):
        row, count = ((0, 1), (3, 1), (1, 2))[part]
        rows = pl.ds(row, count)
        return message(
            layer,
            4 + part,
            own.at[layer, pl.ds(2, 2), rows],
            earlier.at[layer, :, rows],
            later,
        )

    def pass_up(layer):
        return message(layer, 7, earlier.at[layer, :, 0], earlier_below.at[layer], up)

    def pass_down(layer):
        return message(layer, 8, earlier.at[layer, :, 3], earlier_above.at[layer], down)

    def send_rows(layer, half):
        @pl.when(has_up)
        def _():
            to_up(layer, half).start()

        @pl.when(has_down)
        def _():
            to_down(layer, half).start()

    def send_later(layer):
        @pl.when(has_next)
        def _():
            for part in range(3):
                to_later(layer, part).start()

    def clear(taps, frames, row):
        for frame in frames:
            taps[frame, row] = jnp.zeros(taps.shape[2:], taps.dtype)

    def take_rows(layer, taps, half):
        frames = range(2 * half, 2 * half + 2)

        @pl.when(has_up)
        def _():
            to_down(layer, half).wait_recv()
            for f in frames:
                spread(taps, f + 2, 0, above[layer, f].astype(jnp.float32))

        @pl.when(has_down)
        def _():
            to_up(layer, half).wait_recv()
            for f in frames:
                spread(taps, f + 2, 5, below[layer, f].astype(jnp.float32))

    def clear_edges(taps):
        @pl.when(jnp.logical_not(has_up))
        def _():
            clear(taps, range(6), 0)

        @pl.when(jnp.logical_not(has_down))
        def _():
            clear(taps, range(6), 5)

    def pass_on(layer):
        @pl.when(has_prev)
        def _():
            to_later(layer, 0).wait_recv()

            @pl.when(has_up)
            def _():
                pass_up(layer).start()

            to_later(layer, 1).wait_recv()

            @pl.when(has_down)
            def _():
                pass_down(layer).start()

    def add_earlier(layer, taps, weights):
        @pl.when(has_prev)
        def _():
            for r in (0, 3):
                for f in range(2):
                    spread(taps, f, r + 1, earlier[layer, f, r].astype(jnp.float32))
            to_later(layer, 2).wait_recv()
            for r in (1, 2):
                for f in range(2):
                    spread(taps, f, r + 1, earlier[layer, f, r].astype(jnp.float32))
            for f in (-2, -1):
                add_frame(total, taps, weights, f, ROW_PAIRS[0])

            @pl.when(has_up)
            def _():
                pass_down(layer).wait_recv()
                for f in range(2):
                    spread(taps, f, 0, earlier_above[layer, f].astype(jnp.float32))

            @pl.when(has_down)
            def _():
                pass_up(layer).wait_recv()
                for f in range(2):
                    spread(taps, f, 5, earlier_below[layer, f].astype(jnp.float32))

            for f in (-2, -1):
                add_frame(total, taps, weights, f, ROW_PAIRS[1])

    def start_total(bias):
        for f in range(4):
            for r in range(4):
                total[f, r] = jnp.broadcast_to(bias, total.shape[2:])

    gain = vectors[:, 0:1]
    for f in (2, 3, 0, 1):
        for r in range(4):
            act = activate(features[f, r].astype(jnp.float32), gain)
            own[0, f, r] = act.astype(jnp.bfloat16)
            spread(taps_a, f + 2, r + 1, act)

    pl.semaphore_wait(
        barrier,
        sum(present.astype(jnp.int32) for present, _ in neighbours),
    )
    send_rows(0, 1)
    send_rows(0, 0)
    send_later(0)

    width = first_weight.shape[1] // 3
    rows = first_weight.shape[0]
    for p in range(3):
        weights_a[p * rows : (p + 1) * rows, :] = first_weight[:, p * width : (p + 1) * width]
    for p in range(3):
        weights_b[p * rows : (p + 1) * rows, :] = second_weight[:, p * width : (p + 1) * width]

    start_total(vectors[:, 1:2])
    clear_edges(taps_a)
    clear_edges(taps_b)
    for f in range(4):
        add_frame(total, taps_a, weights_a, f, ROW_PAIRS[0])
    take_rows(0, taps_a, 1)
    take_rows(0, taps_a, 0)
    for f in range(4):
        add_frame(total, taps_a, weights_a, f, ROW_PAIRS[1])
    pass_on(0)

    gain = vectors[:, 2:3]

    def second_activation(frames):
        for f in frames:
            for r in range(4):
                act = activate(total[f, r], gain)
                own[1, f, r] = act.astype(jnp.bfloat16)
                spread(taps_b, f + 2, r + 1, act)

    second_activation((2, 3))
    send_later(1)
    send_rows(1, 1)
    add_earlier(0, taps_a, weights_a)
    second_activation((0, 1))
    send_rows(1, 0)

    start_total(vectors[:, 3:4])
    for f in range(4):
        add_frame(total, taps_b, weights_b, f, ROW_PAIRS[0])
    take_rows(1, taps_b, 1)
    take_rows(1, taps_b, 0)
    pass_on(1)
    for f in range(4):
        add_frame(total, taps_b, weights_b, f, ROW_PAIRS[1])

    def finish(frames):
        for f in frames:
            for r in range(4):
                out[f, r] = (features[f, r].astype(jnp.float32) + total[f, r]).astype(
                    jnp.bfloat16
                )

    finish((2, 3))
    add_earlier(1, taps_b, weights_b)
    finish((0, 1))

    for layer in range(2):

        @pl.when(has_up)
        def _():
            for half in range(2):
                to_up(layer, half).wait_send()

        @pl.when(has_down)
        def _():
            for half in range(2):
                to_down(layer, half).wait_send()

        @pl.when(has_next)
        def _():
            for part in range(3):
                to_later(layer, part).wait_send()

        @pl.when(has_prev & has_up)
        def _():
            pass_up(layer).wait_send()

        @pl.when(has_prev & has_down)
        def _():
            pass_down(layer).wait_send()


def local(features, first_gain, first_weight, first_bias, second_gain, second_weight, second_bias):
    channels, frames, rows, columns = features.shape
    by_row = jnp.transpose(features, (1, 2, 0, 3))
    vectors = jnp.stack([first_gain, first_bias, second_gain, second_bias], axis=1)
    vmem = pl.BlockSpec(memory_space=pltpu.VMEM)
    act = jnp.bfloat16
    stacked = (3 * channels, first_weight.shape[1] // 3)
    cells = 2 * channels * first_weight.shape[1] * frames * rows * columns
    result = pl.pallas_call(
        functools.partial(kernel, lax.axis_size("tm"), lax.axis_size("height")),
        out_shape=jax.ShapeDtypeStruct(by_row.shape, jnp.bfloat16),
        in_specs=[vmem] * 4,
        out_specs=vmem,
        scratch_shapes=[
            pltpu.VMEM(stacked, act),
            pltpu.VMEM(stacked, act),
            pltpu.VMEM((2, frames, rows, channels, columns), act),
            pltpu.VMEM((2, frames, channels, columns), act),
            pltpu.VMEM((2, frames, channels, columns), act),
            pltpu.VMEM((2, 2, rows, channels, columns), act),
            pltpu.VMEM((2, 2, channels, columns), act),
            pltpu.VMEM((2, 2, channels, columns), act),
            pltpu.VMEM((frames + 2, rows + 2, 3, channels, columns), act),
            pltpu.VMEM((frames + 2, rows + 2, 3, channels, columns), act),
            pltpu.VMEM((frames, rows, channels, columns), jnp.float32),
            pltpu.SemaphoreType.DMA((2, 9)),
            pltpu.SemaphoreType.DMA((2, 9)),
        ],
        compiler_params=pltpu.CompilerParams(
            collective_id=0, has_side_effects=True, vmem_limit_bytes=48 * 1024 * 1024
        ),
        cost_estimate=pl.CostEstimate(
            flops=2 * cells, bytes_accessed=3 * features.size * 2, transcendentals=features.size * 4
        ),
    )(by_row, vectors, first_weight, second_weight)
    return jnp.transpose(result, (2, 0, 1, 3))


def solution(mesh):
    return jax.shard_map(
        local,
        mesh=mesh,
        in_specs=(P(None, "tm", "height", None), P(), P(), P(), P(), P(), P()),
        out_specs=P(None, "tm", "height", None),
        check_vma=False,
    )
```

time: 56.7 us -> 22.4 us (0.40)
  the two profiles are of different devices: /device:TPU:23 before, /device:TPU:15 now
where the time goes in v1:
time: 22.4 us; the launch traced here: 22.2 us
  Pallas kernels  18.2 us (81%)
  local copies, waits for them, and re-layouts  3.19 us (14%)
  other arithmetic  0.77 us (3%)
    pallas_call x1, Pallas kernels, local(): pl.pallas_call(functools.partial(kernel, lax.axis_size('tm'), lax.axis_si...  18.2 us
    unnamed x5, local copies, waits for them, and re-layouts  2.13 us
    transpose x1, local copies, waits for them, and re-layouts, local(): return jnp.transpose(result, (2, 0, 1, 3))  0.95 us
    another operation x1, other arithmetic, local(): jnp.stack([first_gain, first_bias, second_gain, second_bias], axis=1)  0.77 us

profile of v1, /device:TPU:15, one launch (start us, length us, event | category | flops | bytes accessed | tf_op | source)
XLA Modules:
  0.0 22.2 jit_solution(12738849239538330064)
XLA Ops:
  0.0 0.0 copy-start
  0.0 0.8 %pad_maximum_fusion = f32[96,4]{0,1:T(4,128)S(1)} fusion(f32[96,1]{0,1:T(1,128)} %bitcast.10, f32[96,1]{0,1:T(1,128)} %bitcast.11, f32[96,1]{0,1:T(1,128)} %bitcast.12, f32[96,1]{0,1:T(1,128)} %bitcast.13), kind=kLoop, calls=%fused_computation.1 | loop fusion | flops 1152 | bytes 3072 | tf_op jit(solution)/shard_map/stack | solution.py:320
  0.8 0.1 copy.15.vectors
  0.9 1.1 %copy.18 = bf16[96,4,4,128]{3,0,2,1:T(8,128)(2,1)S(1)} copy(bf16[96,4,4,128]{3,2,1,0:T(4,128)(2,1)} %param.7) | data formatting | bytes 786432 | tf_op args[0]
  2.0 0.0 copy-done
  2.0 0.0 copy-start.1
  2.0 1.0 %copy-done.1 = bf16[96,2592]{1,0:T(8,128)(2,1)S(1)} copy-done((bf16[96,2592]{1,0:T(8,128)(2,1)S(1)}, bf16[96,2592]{1,0:T(8,128)(2,1)}, u32[]{:S(2)}) %copy-start.1) | copy-done | bytes 497688
  3.0 18.2 %shard_map.73 = bf16[4,4,96,128]{3,2,1,0:T(8,128)(2,1)S(1)} custom-call(bf16[4,4,96,128]{3,2,1,0:T(8,128)(2,1)S(1)} %bitcast.9, f32[96,4]{1,0:T(8,128)S(1)} %copy.15.vectors, bf16[96,2592]{1,0:T(8,128)(2,1)S(1)} %copy-done, bf16[96,2592]{1,0:T(8,128)(2,1)S(1)} %copy-done.1), custom_call_target="tpu_custom_call" | custom-call | flops 2038431744 | bytes 1179648 | tf_op jit(solution)/shard_map/pallas_call | solution.py:325
  21.2 0.9 %copy.16 = bf16[96,4,4,128]{3,2,1,0:T(4,128)(2,1)} copy(bf16[96,4,4,128]{3,0,2,1:T(8,128)(2,1)S(1)} %bitcast.8) | data formatting | bytes 786432 | tf_op jit(solution)/shard_map/transpose | solution.py:352
Async XLA Ops:
  0.0 2.0 %copy-start = (bf16[96,2592]{1,0:T(8,128)(2,1)S(1)}, bf16[96,2592]{1,0:T(8,128)(2,1)}, u32[]{:S(2)}) copy-start(bf16[96,2592]{1,0:T(8,128)(2,1)} %first_weight.1) | copy-start | bytes 1492996
  2.0 1.0 %copy-start.1 = (bf16[96,2592]{1,0:T(8,128)(2,1)S(1)}, bf16[96,2592]{1,0:T(8,128)(2,1)}, u32[]{:S(2)}) copy-start(bf16[96,2592]{1,0:T(8,128)(2,1)} %second_weight.1) | copy-start | bytes 1492996

commit v2 on v1

--- a/solution.py
+++ b/solution.py
@@ -47,14 +47,27 @@
             ]
 
 
+def column(vectors, i, columns):
+    wide = jnp.broadcast_to(vectors[i], (columns, vectors.shape[2]))
+    return jnp.transpose(wide)
+
+
 def kernel(
     tm_count,
     height_count,
+    features_hbm,
+    first_weight_hbm,
+    second_weight_hbm,
+    first_gain_hbm,
+    first_bias_hbm,
+    second_gain_hbm,
+    second_bias_hbm,
+    out,
     features,
     vectors,
     first_weight,
     second_weight,
-    out,
+    cells,
     weights_a,
     weights_b,
     own,
@@ -68,7 +81,24 @@
     total,
     send_sem,
     recv_sem,
+    load_sem,
 ):
+    loads = [
+        pltpu.make_async_copy(source, target, load_sem.at[i])
+        for i, (source, target) in enumerate(
+            (
+                (features_hbm, features),
+                (first_gain_hbm, vectors.at[0]),
+                (first_bias_hbm, vectors.at[1]),
+                (second_gain_hbm, vectors.at[2]),
+                (second_bias_hbm, vectors.at[3]),
+                (first_weight_hbm, first_weight),
+                (second_weight_hbm, second_weight),
+            )
+        )
+    ]
+    for load in loads:
+        load.start()
     t = lax.axis_index("tm")
     h = lax.axis_index("height")
     has_prev, has_next = t > 0, t < tm_count - 1
@@ -197,7 +227,7 @@
                 for f in range(2):
                     spread(taps, f, r + 1, earlier[layer, f, r].astype(jnp.float32))
             for f in (-2, -1):
-                add_frame(total, taps, weights, f, ROW_PAIRS[0])
+                add_frame(total.at[layer], taps, weights, f, ROW_PAIRS[0])
 
             @pl.when(has_up)
             def _():
@@ -212,17 +242,33 @@
                     spread(taps, f, 5, earlier_below[layer, f].astype(jnp.float32))
 
             for f in (-2, -1):
-                add_frame(total, taps, weights, f, ROW_PAIRS[1])
-
-    def start_total(bias):
+                add_frame(total.at[layer], taps, weights, f, ROW_PAIRS[1])
+
+    def start_total(layer, bias):
         for f in range(4):
             for r in range(4):
-                total[f, r] = jnp.broadcast_to(bias, total.shape[2:])
-
-    gain = vectors[:, 0:1]
+                total[layer, f, r] = bias
+
+    def add_own(layer, taps, weights, frames, pair):
+        for f in frames:
+            add_frame(total.at[layer], taps, weights, f, ROW_PAIRS[pair])
+
+    def feature_row(f, r):
+        return cells[f, pl.ds(r, channels, stride=4), :]
+
+    channels, columns = total.shape[3:]
+    for load in loads[1:5]:
+        load.wait()
+    first_gain, first_bias, second_gain, second_bias = (
+        column(vectors, i, columns) for i in range(4)
+    )
+
+    loads[0].wait()
+    for f in range(4):
+        cells[f] = features[:, f].astype(jnp.float32).reshape(4 * channels, columns)
     for f in (2, 3, 0, 1):
         for r in range(4):
-            act = activate(features[f, r].astype(jnp.float32), gain)
+            act = activate(feature_row(f, r), first_gain)
             own[0, f, r] = act.astype(jnp.bfloat16)
             spread(taps_a, f + 2, r + 1, act)
 
@@ -234,56 +280,52 @@
     send_rows(0, 0)
     send_later(0)
 
-    width = first_weight.shape[1] // 3
-    rows = first_weight.shape[0]
-    for p in range(3):
-        weights_a[p * rows : (p + 1) * rows, :] = first_weight[:, p * width : (p + 1) * width]
-    for p in range(3):
-        weights_b[p * rows : (p + 1) * rows, :] = second_weight[:, p * width : (p + 1) * width]
-
-    start_total(vectors[:, 1:2])
+    def stack(weights, source):
+        width = source.shape[1] // 3
+        for p in range(3):
+            weights[p * channels : (p + 1) * channels, :] = source[:, p * width : (p + 1) * width]
+
+    loads[5].wait()
+    stack(weights_a, first_weight)
+    start_total(0, first_bias)
     clear_edges(taps_a)
-    clear_edges(taps_b)
-    for f in range(4):
-        add_frame(total, taps_a, weights_a, f, ROW_PAIRS[0])
+    add_own(0, taps_a, weights_a, range(4), 0)
     take_rows(0, taps_a, 1)
     take_rows(0, taps_a, 0)
-    for f in range(4):
-        add_frame(total, taps_a, weights_a, f, ROW_PAIRS[1])
-    pass_on(0)
-
-    gain = vectors[:, 2:3]
+    add_own(0, taps_a, weights_a, range(4), 1)
 
     def second_activation(frames):
         for f in frames:
             for r in range(4):
-                act = activate(total[f, r], gain)
+                act = activate(total[0, f, r], second_gain)
                 own[1, f, r] = act.astype(jnp.bfloat16)
                 spread(taps_b, f + 2, r + 1, act)
+
+    def finish(frames):
+        for f in frames:
+            for r in range(4):
+                out[f, r] = (feature_row(f, r) + total[1, f, r]).astype(jnp.bfloat16)
 
     second_activation((2, 3))
     send_later(1)
     send_rows(1, 1)
+    pass_on(0)
+
+    loads[6].wait()
+    stack(weights_b, second_weight)
+    start_total(1, second_bias)
+    clear_edges(taps_b)
+    add_own(1, taps_b, weights_b, (2, 3), 0)
+    take_rows(1, taps_b, 1)
+    add_own(1, taps_b, weights_b, (2, 3), 1)
+
     add_earlier(0, taps_a, weights_a)
     second_activation((0, 1))
     send_rows(1, 0)
-
-    start_total(vectors[:, 3:4])
-    for f in range(4):
-        add_frame(total, taps_b, weights_b, f, ROW_PAIRS[0])
-    take_rows(1, taps_b, 1)
+    add_own(1, taps_b, weights_b, (0, 1), 0)
+    pass_on(1)
     take_rows(1, taps_b, 0)
-    pass_on(1)
-    for f in range(4):
-        add_frame(total, taps_b, weights_b, f, ROW_PAIRS[1])
-
-    def finish(frames):
-        for f in frames:
-            for r in range(4):
-                out[f, r] = (features[f, r].astype(jnp.float32) + total[f, r]).astype(
-                    jnp.bfloat16
-                )
-
+    add_own(1, taps_b, weights_b, (0, 1), 1)
     finish((2, 3))
     add_earlier(1, taps_b, weights_b)
     finish((0, 1))
@@ -316,18 +358,22 @@
 
 def local(features, first_gain, first_weight, first_bias, second_gain, second_weight, second_bias):
     channels, frames, rows, columns = features.shape
-    by_row = jnp.transpose(features, (1, 2, 0, 3))
-    vectors = jnp.stack([first_gain, first_bias, second_gain, second_bias], axis=1)
+    vectors = [v.reshape(1, channels) for v in (first_gain, first_bias, second_gain, second_bias)]
     vmem = pl.BlockSpec(memory_space=pltpu.VMEM)
     act = jnp.bfloat16
     stacked = (3 * channels, first_weight.shape[1] // 3)
     cells = 2 * channels * first_weight.shape[1] * frames * rows * columns
     result = pl.pallas_call(
         functools.partial(kernel, lax.axis_size("tm"), lax.axis_size("height")),
-        out_shape=jax.ShapeDtypeStruct(by_row.shape, jnp.bfloat16),
-        in_specs=[vmem] * 4,
+        out_shape=jax.ShapeDtypeStruct((frames, rows, channels, columns), jnp.bfloat16),
+        in_specs=[pl.BlockSpec(memory_space=pl.ANY)] * 7,
         out_specs=vmem,
         scratch_shapes=[
+            pltpu.VMEM(features.shape, act),
+            pltpu.VMEM((4, 1, channels), jnp.float32),
+            pltpu.VMEM(first_weight.shape, act),
+            pltpu.VMEM(second_weight.shape, act),
+            pltpu.VMEM((frames, rows * channels, columns), jnp.float32),
             pltpu.VMEM(stacked, act),
             pltpu.VMEM(stacked, act),
             pltpu.VMEM((2, frames, rows, channels, columns), act),
@@ -338,17 +384,18 @@
             pltpu.VMEM((2, 2, channels, columns), act),
             pltpu.VMEM((frames + 2, rows + 2, 3, channels, columns), act),
             pltpu.VMEM((frames + 2, rows + 2, 3, channels, columns), act),
-            pltpu.VMEM((frames, rows, channels, columns), jnp.float32),
+            pltpu.VMEM((2, frames, rows, channels, columns), jnp.float32),
             pltpu.SemaphoreType.DMA((2, 9)),
             pltpu.SemaphoreType.DMA((2, 9)),
+            pltpu.SemaphoreType.DMA((7,)),
         ],
         compiler_params=pltpu.CompilerParams(
-            collective_id=0, has_side_effects=True, vmem_limit_bytes=48 * 1024 * 1024
+            collective_id=0, has_side_effects=True, vmem_limit_bytes=56 * 1024 * 1024
         ),
         cost_estimate=pl.CostEstimate(
             flops=2 * cells, bytes_accessed=3 * features.size * 2, transcendentals=features.size * 4
         ),
-    )(by_row, vectors, first_weight, second_weight)
+    )(features, first_weight, second_weight, *vectors)
     return jnp.transpose(result, (2, 0, 1, 3))
 
 

time: 22.4 us -> 21.5 us (0.960)
  the two profiles are of different devices: /device:TPU:15 before, /device:TPU:11 now
where the time goes in v2:
time: 21.5 us; the launch traced here: 21.3 us
  Pallas kernels  19.4 us (90%)
  local copies, waits for them, and re-layouts  1.94 us (9%)
    pallas_call x1, Pallas kernels, local(): pl.pallas_call(functools.partial(kernel, lax.axis_size('tm'), lax.axis_si...  19.4 us
    transpose x1, local copies, waits for them, and re-layouts, local(): return jnp.transpose(result, (2, 0, 1, 3))  1.94 us

profile of v2, /device:TPU:11, one launch (start us, length us, event | category | flops | bytes accessed | tf_op | source)
XLA Modules:
  0.0 21.3 jit_solution(13003565050755237417)
XLA Ops:
  0.0 19.4 %shard_map.73 = bf16[4,4,96,128]{3,2,1,0:T(8,128)(2,1)} custom-call(bf16[96,4,4,128]{3,2,1,0:T(4,128)(2,1)} %features_hbm.1, bf16[96,2592]{1,0:T(8,128)(2,1)} %first_weight_hbm.1, bf16[96,2592]{1,0:T(8,128)(2,1)} %second_weight_hbm.1, f32[1,96]{1,0:T(1,128)} %bitcast.6, f32[1,96]{1,0:T(1,128)} %bitcast.7, f32[1,96]{1,0:T(1,128)} %bitcast.8, f32[1,96]{1,0:T(1,128)} %bitcast.9), custom_call_target="tpu_custom_call" | custom-call | flops 2038431744 | bytes 1179648 | tf_op jit(solution)/shard_map/pallas_call | solution.py:366
  19.4 1.9 %copy.8 = bf16[96,4,4,128]{3,2,1,0:T(4,128)(2,1)} copy(bf16[96,4,4,128]{3,0,2,1:T(8,128)(2,1)} %bitcast.5) | data formatting | bytes 786432 | tf_op jit(solution)/shard_map/transpose | solution.py:399

commit v3 on v2

--- a/solution.py
+++ b/solution.py
@@ -14,23 +14,23 @@
 def activate(values, gain):
     mean_square = jnp.mean(values * values, axis=0, keepdims=True)
     scaled = values * lax.rsqrt(mean_square + 1e-06) * gain
-    return scaled / (1.0 + jnp.exp(-scaled))
+    return scaled * (0.5 + 0.5 * jnp.tanh(0.5 * scaled))
 
 
 def spread(taps, frame, row, values):
+    values = values.astype(jnp.bfloat16)
     lanes = lax.broadcasted_iota(jnp.int32, values.shape, 1)
     last = values.shape[1] - 1
-    before = jnp.where(lanes == 0, 0.0, pltpu.roll(values, 1, 1))
-    after = jnp.where(lanes == last, 0.0, pltpu.roll(values, last, 1))
-    taps[frame, row, 0] = before.astype(jnp.bfloat16)
-    taps[frame, row, 1] = values.astype(jnp.bfloat16)
-    taps[frame, row, 2] = after.astype(jnp.bfloat16)
-
-
-def add_frame(total, taps, weights, frame, pair):
+    zero = jnp.zeros_like(values)
+    taps[frame, row, 0] = jnp.where(lanes == 0, zero, pltpu.roll(values, 1, 1))
+    taps[frame, row, 1] = values
+    taps[frame, row, 2] = jnp.where(lanes == last, zero, pltpu.roll(values, last, 1))
+
+
+def add_frame(total, taps, weights, frame, pair, targets=range(4)):
     channels = taps.shape[3]
     columns = taps.shape[4]
-    reached = [(tap, frame + 2 - tap) for tap in range(3) if 0 <= frame + 2 - tap < 4]
+    reached = [(tap, frame + 2 - tap) for tap in range(3) if frame + 2 - tap in targets]
     low = reached[0][0] * channels
     right = jnp.concatenate(
         [taps[frame + 2, r : r + 3].reshape(9 * channels, columns) for r in pair], axis=1
@@ -167,10 +167,10 @@
         def _():
             to_down(layer, half).start()
 
-    def send_later(layer):
+    def send_later(layer, parts):
         @pl.when(has_next)
         def _():
-            for part in range(3):
+            for part in parts:
                 to_later(layer, part).start()
 
     def clear(taps, frames, row):
@@ -219,11 +219,8 @@
     def add_earlier(layer, taps, weights):
         @pl.when(has_prev)
         def _():
-            for r in (0, 3):
-                for f in range(2):
-                    spread(taps, f, r + 1, earlier[layer, f, r].astype(jnp.float32))
             to_later(layer, 2).wait_recv()
-            for r in (1, 2):
+            for r in range(4):
                 for f in range(2):
                     spread(taps, f, r + 1, earlier[layer, f, r].astype(jnp.float32))
             for f in (-2, -1):
@@ -249,9 +246,9 @@
             for r in range(4):
                 total[layer, f, r] = bias
 
-    def add_own(layer, taps, weights, frames, pair):
+    def add_own(layer, taps, weights, frames, pair, targets=range(4)):
         for f in frames:
-            add_frame(total.at[layer], taps, weights, f, ROW_PAIRS[pair])
+            add_frame(total.at[layer], taps, weights, f, ROW_PAIRS[pair], targets)
 
     def feature_row(f, r):
         return cells[f, pl.ds(r, channels, stride=4), :]
@@ -278,7 +275,7 @@
     )
     send_rows(0, 1)
     send_rows(0, 0)
-    send_later(0)
+    send_later(0, (0, 1, 2))
 
     def stack(weights, source):
         width = source.shape[1] // 3
@@ -289,14 +286,10 @@
     stack(weights_a, first_weight)
     start_total(0, first_bias)
     clear_edges(taps_a)
-    add_own(0, taps_a, weights_a, range(4), 0)
-    take_rows(0, taps_a, 1)
-    take_rows(0, taps_a, 0)
-    add_own(0, taps_a, weights_a, range(4), 1)
-
-    def second_activation(frames):
+
+    def second_activation(frames, rows):
         for f in frames:
-            for r in range(4):
+            for r in rows:
                 act = activate(total[0, f, r], second_gain)
                 own[1, f, r] = act.astype(jnp.bfloat16)
                 spread(taps_b, f + 2, r + 1, act)
@@ -304,12 +297,21 @@
     def finish(frames):
         for f in frames:
             for r in range(4):
-                out[f, r] = (feature_row(f, r) + total[1, f, r]).astype(jnp.bfloat16)
-
-    second_activation((2, 3))
-    send_later(1)
+                cells[f, pl.ds(r, channels, stride=4), :] = feature_row(f, r) + total[1, f, r]
+            out[:, f] = cells[f].reshape(channels, 4, columns).astype(jnp.bfloat16)
+
+    add_own(0, taps_a, weights_a, range(4), 0, (2, 3))
+    second_activation((2, 3), (1, 2))
+    send_later(1, (2,))
+    take_rows(0, taps_a, 1)
+    take_rows(0, taps_a, 0)
+    add_own(0, taps_a, weights_a, range(4), 1, (2, 3))
+    second_activation((2, 3), (0, 3))
+    send_later(1, (0, 1))
     send_rows(1, 1)
     pass_on(0)
+    add_own(0, taps_a, weights_a, (0, 1), 0, (0, 1))
+    add_own(0, taps_a, weights_a, (0, 1), 1, (0, 1))
 
     loads[6].wait()
     stack(weights_b, second_weight)
@@ -320,7 +322,7 @@
     add_own(1, taps_b, weights_b, (2, 3), 1)
 
     add_earlier(0, taps_a, weights_a)
-    second_activation((0, 1))
+    second_activation((0, 1), range(4))
     send_rows(1, 0)
     add_own(1, taps_b, weights_b, (0, 1), 0)
     pass_on(1)
@@ -363,10 +365,10 @@
     act = jnp.bfloat16
     stacked = (3 * channels, first_weight.shape[1] // 3)
     cells = 2 * channels * first_weight.shape[1] * frames * rows * columns
-    result = pl.pallas_call(
+    return pl.pallas_call(
         functools.partial(kernel, lax.axis_size("tm"), lax.axis_size("height")),
-        out_shape=jax.ShapeDtypeStruct((frames, rows, channels, columns), jnp.bfloat16),
-        in_specs=[pl.BlockSpec(memory_space=pl.ANY)] * 7,
+        out_shape=jax.ShapeDtypeStruct(features.shape, jnp.bfloat16),
+        in_specs=[pl.BlockSpec(memory_space=pltpu.HBM)] * 7,
         out_specs=vmem,
         scratch_shapes=[
             pltpu.VMEM(features.shape, act),
@@ -396,7 +398,6 @@
             flops=2 * cells, bytes_accessed=3 * features.size * 2, transcendentals=features.size * 4
         ),
     )(features, first_weight, second_weight, *vectors)
-    return jnp.transpose(result, (2, 0, 1, 3))
 
 
 def solution(mesh):

time: 21.5 us -> 21.1 us (0.981)
  Pallas kernels: 19.4 us -> 19 us
    transpose x1 -> x0, local copies, waits for them, and re-layouts: 1.94 us -> none  [local(): return jnp.transpose(result, (2, 0, 1, 3))]
    unnamed x0 -> x1, local copies, waits for them, and re-layouts: none -> 1.88 us
    pallas_call x1, Pallas kernels: 19.4 us -> 19 us  [local(): pl.pallas_call(functools.partial(kernel, lax.axis_size('tm'), lax.axis_si...]
where the time goes in v3:
time: 21.1 us; the launch traced here: 20.9 us
  Pallas kernels  19 us (90%)
  local copies, waits for them, and re-layouts  1.88 us (9%)
    pallas_call x1, Pallas kernels, local(): pl.pallas_call(functools.partial(kernel, lax.axis_size('tm'), lax.axis_si...  19 us
    unnamed x1, local copies, waits for them, and re-layouts  1.88 us

profile of v3, /device:TPU:11, one launch (start us, length us, event | category | flops | bytes accessed | tf_op | source)
XLA Modules:
  0.0 20.9 jit_solution(7474244148312798735)
XLA Ops:
  0.0 19.0 %shard_map.73 = bf16[96,4,4,128]{3,2,1,0:T(4,128)(2,1)} custom-call(bf16[96,4,4,128]{3,2,1,0:T(4,128)(2,1)} %features_hbm.1, bf16[96,2592]{1,0:T(8,128)(2,1)} %first_weight_hbm.1, bf16[96,2592]{1,0:T(8,128)(2,1)} %second_weight_hbm.1, f32[1,96]{1,0:T(1,128)} %bitcast.4, f32[1,96]{1,0:T(1,128)} %bitcast.5, f32[1,96]{1,0:T(1,128)} %bitcast.6, f32[1,96]{1,0:T(1,128)} %bitcast.7), custom_call_target="tpu_custom_call" | custom-call | flops 2038431744 | bytes 1179648 | tf_op jit(solution)/shard_map/pallas_call | solution.py:368
  19.0 1.9 %copy.9 = bf16[96,4,4,128]{3,2,1,0:T(4,128)(2,1)} copy(bf16[96,4,4,128]{3,2,1,0:T(4,128)(2,1)} %shard_map.73) | data formatting | bytes 786432
